TPU v7x, 512 devices: a whole 4x8x8 slice. The times are simulated.
512 devices in a mesh: dp: 32 (over y_lo, z), tensor: 16 (over y_hi, x, core).
Axes of the slice: x: 4, y: 8 (y_hi: 2, y_lo: 4; y = y_hi * 4 + y_lo), z: 8, core: 2. Of those that a mesh axis runs over, the one named last changes fastest.
Arguments:
- hidden: bfloat16 [4096, 16384], P('dp', 'tensor'), may hold values from -6 to 6
- down_weight: bfloat16 [16384, 4096], P('tensor', 'dp'), may hold values from -0.046875 to 0.046875
- factor_a: bfloat16 [1024, 16384], P('dp', 'tensor'), may hold values from -0.046875 to 0.046875
- factor_b: bfloat16 [1024, 4096], P('dp', 'tensor'), may hold values from -0.375 to 0.375
- cotangent: bfloat16 [4096, 4096], P('dp', 'tensor'), may hold values from -6 to 6
- block_job: int32 [64, 1], P('dp'), may hold values from 0 to 3
- ranks: int32 [4], replicated, may hold values from 64 to 256, as said below
Outputs:
- mixed: bfloat16 [4096, 4096], P('dp', 'tensor')
- hidden_grad: bfloat16 [4096, 16384], P('dp', 'tensor')
- grad_a: bfloat16 [1024, 16384], P('dp', 'tensor')
- grad_b: bfloat16 [1024, 4096], P('dp', 'tensor')
Inputs may be any that keep to these rules, and one draw needn't show every extreme that they name: `ranks`: every job uses a multiple of 64 rank slots, and each multiple from 64 to 256 is used by one job.
All inputs are finite; a program needn't handle non-finite values.
Results may differ from a plain program's by a relative error of at most 0.022.
Values may be sent and summed in bfloat16 or wider, within the bound.
A program may use at most 64 MiB of HBM per device.

v0:
```python
import jax
import jax.numpy as jnp
from jax import lax
from jax.sharding import PartitionSpec as P

R = 256
JOBS = 4
BLOCK = 64


adapter_scale = 2.0


def combine_rows(partial_value, keep_mask):
    return lax.psum(partial_value * keep_mask, "tensor")


def on_device(hidden, down_weight, factor_a, factor_b, cotangent, block_job, ranks):
    tok_rows = hidden.shape[0]
    gathered_a, gathered_b = (
        lax.all_gather(factor_a, "dp", axis=0, tiled=True),
        lax.all_gather(factor_b, "dp", axis=0, tiled=True),
    )
    token_job = jnp.repeat(block_job[:, 0], BLOCK)
    job_index = jnp.arange(JOBS, dtype=jnp.int32)
    onehot = (token_job[:, None] == job_index[None, :]).astype(jnp.float32)
    token_rank = jnp.sum(onehot * ranks[None, :].astype(jnp.float32), axis=1)
    rank_index = jnp.arange(R, dtype=jnp.float32)
    rank_keep = (rank_index[None, :] < token_rank[:, None]).astype(jnp.float32)
    keep_mask = (onehot[:, :, None] * rank_keep[:, None, :]).reshape(tok_rows, JOBS * R)
    cotangent_all = lax.all_gather(cotangent, "tensor", axis=1, tiled=True)
    contract_last = (((1,), (1,)), ((), ()))
    weight_all = lax.all_gather(down_weight, "dp", axis=1, tiled=True)
    frozen_out = jnp.dot(hidden, weight_all, preferred_element_type=jnp.float32)
    frozen_grad = lax.dot_general(
        cotangent_all, weight_all, contract_last, preferred_element_type=jnp.float32
    )
    frozen = lax.psum_scatter(
        frozen_out.astype(jnp.bfloat16), "tensor", scatter_dimension=1, tiled=True
    ).astype(jnp.float32)
    delta_part = lax.dot_general(
        hidden, gathered_a, contract_last, preferred_element_type=jnp.float32
    )
    delta = combine_rows(delta_part, keep_mask)
    delta_low = delta.astype(jnp.bfloat16)
    mixed = (
        frozen + adapter_scale * jnp.dot(delta_low, gathered_b, preferred_element_type=jnp.float32)
    ).astype(jnp.bfloat16)
    grad_part = lax.dot_general(
        cotangent, gathered_b, contract_last, preferred_element_type=jnp.float32
    )
    grad_delta = combine_rows(grad_part, keep_mask)
    grad_low = grad_delta.astype(jnp.bfloat16)
    hidden_grad = (
        frozen_grad
        + adapter_scale * jnp.dot(grad_low, gathered_a, preferred_element_type=jnp.float32)
    ).astype(jnp.bfloat16)
    contract_first = (((0,), (0,)), ((), ()))
    picked = grad_low
    grad_first = lax.psum_scatter(
        (
            adapter_scale
            * lax.dot_general(picked, hidden, contract_first, preferred_element_type=jnp.float32)
        ).astype(jnp.bfloat16),
        "dp",
        scatter_dimension=0,
        tiled=True,
    )
    picked = delta_low
    grad_second = lax.psum_scatter(
        (
            adapter_scale
            * lax.dot_general(picked, cotangent, contract_first, preferred_element_type=jnp.float32)
        ).astype(jnp.bfloat16),
        "dp",
        scatter_dimension=0,
        tiled=True,
    )
    return (mixed, hidden_grad, grad_first, grad_second)


def solution(mesh):
    in_specs = (
        P("dp", "tensor"),
        P("tensor", "dp"),
        P("dp", "tensor"),
        P("dp", "tensor"),
        P("dp", "tensor"),
        P("dp", None),
        P(),
    )
    out_specs = (P("dp", "tensor"), P("dp", "tensor"), P("dp", "tensor"), P("dp", "tensor"))
    return jax.shard_map(
        on_device, mesh=mesh, in_specs=in_specs, out_specs=out_specs, check_vma=False
    )
```

profile of v0, /device:TPU:6, one launch (start us, length us, event | category | flops | bytes accessed | tf_op | source)
XLA Modules:
  0.0 825.5 jit_solution(8608715986102523611)
XLA Ops:
  7.2 0.0 copy-start
  7.2 0.0 all-gather.4.cloned.1.call-start
  7.2 0.7 all-gather.4.cloned.1.call-update
  7.9 0.0 all-gather.6.cloned.1.call-start
  8.0 0.7 all-gather.6.cloned.1.call-update
  8.7 0.0 all-gather.8.cloned.1.call-start
  8.7 0.7 all-gather.8.cloned.1.call-update
  9.4 0.0 reduce-scatter.4.cloned.1.call-start
  9.4 0.7 convert_element_type.45
  10.1 0.7 broadcast_in_dim.2
  10.8 0.1 eq.19
  10.9 0.2 select_reduce_fusion
  11.1 0.1 fusion.10
  11.2 0.1 fusion.9
  11.3 0.2 broadcast_multiply_fusion
  11.5 0.1 copy.11
  11.6 0.0 copy-start.3
  11.6 0.0 copy-start.2
  11.6 176.5 %all-gather.4.cloned.1.call-done = bf16[1024,4096]{1,0:T(8,128)(2,1)} async-done(((bf16[1024,128]{1,0:T(8,128)(2,1)}), bf16[1024,4096]{1,0:T(8,128)(2,1)}) %all-gather.4.cloned.1.call-update) | async-done | bytes 8388624 | tf_op jit(solution)/shard_map/all_gather | solution.py:33
  188.2 0.0 copy-done
  188.2 5.7 convolution_convert_fusion
  193.8 0.0 reduce-scatter.4.cloned.1.call-update
  193.9 0.0 reduce-scatter.8.cloned.1.call-start
  193.9 0.0 copy-done.3
  193.9 80.0 %all_gather.14 = bf16[1024,256]{1,0:T(8,128)(2,1)S(1)} all-gather(bf16[32,256]{1,0:T(8,128)(2,1)S(1)} %copy-done.3), channel_id=1, replica_groups=mesh['dp'=32,'tensor'=16] {'dp'}, dimensions={0}, use_global_device_ids=true | all-gather | bytes 540672 | tf_op jit(solution)/shard_map/all_gather | solution.py:22
  273.9 0.0 copy-done.2
  273.9 0.3 convolution_multiply_fusion.2
  274.2 70.8 %all-gather.6.cloned.1.call-done = bf16[1024,1024]{1,0:T(8,128)(2,1)} async-done(((bf16[32,1024]{1,0:T(8,128)(2,1)}), bf16[1024,1024]{1,0:T(8,128)(2,1)}) %all-gather.6.cloned.1.call-update) | async-done | bytes 2097168 | tf_op jit(solution)/shard_map/all_gather | solution.py:21
  345.0 2.4 convolution_multiply_fusion.3
  347.4 92.6 %all-reduce.2 = (bf16[128,1024]{1,0:T(8,128)(2,1)S(1)}, bf16[128,1024]{1,0:T(8,128)(2,1)S(1)}) all-reduce(f32[128,1024]{1,0:T(8,128)S(1)} %convolution_multiply_fusion.3, f32[128,1024]{1,0:T(8,128)S(1)} %convolution_multiply_fusion.2), channel_id=1, replica_groups=mesh['dp'=32,'tensor'=16] {'tensor'}, use_global_device_ids=true, to_apply=%region_2.0 | all-reduce | flops 262144 | bytes 1572864 | tf_op jit(solution)/shard_map/psum | solution.py:15
  440.0 1.1 fusion
  441.2 0.0 reduce-scatter.8.cloned.1.call-update
  441.2 0.0 reduce-scatter.6.cloned.1.call-start
  441.3 2.1 multiply_convert_fusion
  443.3 0.0 reduce-scatter.6.cloned.1.call-update
  443.3 0.0 copy-start.1
  443.4 0.0 all-gather.8.cloned.1.call-done
  443.4 6.7 fusion.11
  450.1 0.0 copy-done.1
  450.1 1.2 fusion.2
  451.3 43.9 %reduce-scatter.4.cloned.1.call-done = bf16[128,256]{1,0:T(8,128)(2,1)} async-done(((bf16[128,4096]{1,0:T(8,128)(2,1)}), bf16[128,256]{1,0:T(8,128)(2,1)}) %reduce-scatter.4.cloned.1.call-update) | async-done | bytes 65552 | tf_op jit(solution)/shard_map/reduce_scatter | solution.py:38
  495.2 1.7 fusion.4
  496.9 160.3 %reduce-scatter.8.cloned.1.call-done = bf16[32,256]{1,0:T(8,128)(2,1)} async-done(((bf16[1024,256]{1,0:T(8,128)(2,1)}), bf16[32,256]{1,0:T(8,128)(2,1)}) %reduce-scatter.8.cloned.1.call-update) | async-done | bytes 16400 | tf_op jit(solution)/shard_map/reduce_scatter | solution.py:70
  657.3 161.4 %reduce-scatter.6.cloned.1.call-done = bf16[32,1024]{1,0:T(8,128)(2,1)} async-done(((bf16[1024,1024]{1,0:T(8,128)(2,1)}), bf16[32,1024]{1,0:T(8,128)(2,1)}) %reduce-scatter.6.cloned.1.call-update) | async-done | bytes 65552 | tf_op jit(solution)/shard_map/reduce_scatter | solution.py:60
Async XLA Ops:
  7.2 181.0 %copy-start = (bf16[128,1024]{1,0:T(8,128)(2,1)S(1)}, bf16[128,1024]{1,0:T(8,128)(2,1)}, u32[]{:S(2)}) copy-start(bf16[128,1024]{1,0:T(8,128)(2,1)} %param.7) | copy-start | bytes 786436
  7.2 181.0 %all-gather.4.cloned.1.call-start = ((), (), s32[]{:S(2)}) async-start(), calls=%async_computation.3 | async-start | bytes 8650752 | tf_op jit(solution)/shard_map/all_gather | solution.py:33
  7.9 337.1 %all-gather.6.cloned.1.call-start = ((), (), s32[]{:S(2)}) async-start(), calls=%async_computation.5 | async-start | bytes 2162688 | tf_op jit(solution)/shard_map/all_gather | solution.py:21
  8.7 434.7 %all-gather.8.cloned.1.call-start = ((), (), s32[]{:S(2)}) async-start(), calls=%async_computation.6 | async-start | bytes 1114112 | tf_op jit(solution)/shard_map/all_gather | solution.py:31
  9.4 485.8 %reduce-scatter.4.cloned.1.call-start = ((), (), s32[]{:S(2)}) async-start(), calls=%async_computation.4 | async-start | bytes 1114112 | tf_op jit(solution)/shard_map/reduce_scatter | solution.py:38
  11.6 182.3 %copy-start.3 = (bf16[32,256]{1,0:T(8,128)(2,1)S(1)}, bf16[32,256]{1,0:T(8,128)(2,1)}, u32[]{:S(2)}) copy-start(bf16[32,256]{1,0:T(8,128)(2,1)} %param.10) | copy-start | bytes 49156
  11.6 262.3 %copy-start.2 = (bf16[128,256]{1,0:T(8,128)(2,1)S(1)}, bf16[128,256]{1,0:T(8,128)(2,1)}, u32[]{:S(2)}) copy-start(bf16[128,256]{1,0:T(8,128)(2,1)} %param.11) | copy-start | bytes 196612
  193.9 463.4 %reduce-scatter.8.cloned.1.call-start = ((), (), s32[]{:S(2)}) async-start(), calls=%async_computation.8 | async-start | bytes 540672 | tf_op jit(solution)/shard_map/reduce_scatter | solution.py:70
  441.2 377.5 %reduce-scatter.6.cloned.1.call-start = ((), (), s32[]{:S(2)}) async-start(), calls=%async_computation.7 | async-start | bytes 2162688 | tf_op jit(solution)/shard_map/reduce_scatter | solution.py:60
  443.3 6.8 copy-start.1
Sparse Core Ops, SparseCore 0:
  10.0 178.0 all-gather.3
  190.2 154.7 all-gather.5
  348.1 56.2 all-gather.7
  409.0 86.2 reduce-scatter.3
  498.7 158.5 reduce-scatter.7
  660.5 158.1 reduce-scatter.5
where the time goes:
time: 826 us
  waiting for transfers between devices  615 us (74%)
  blocking collectives  173 us (21%)
  matrix products  21.2 us (3%)
  between operations  14.2 us (2%)
    all_gather x1, waiting for transfers between devices, on_device(): weight_all = lax.all_gather(down_weight, 'dp', axis=1, tiled=True)  177 us
    reduce_scatter x1, waiting for transfers between devices, on_device(): lax.psum_scatter((adapter_scale * lax.dot_general(picked, hidden, contrac...  161 us
    reduce_scatter x1, waiting for transfers between devices, on_device(): lax.psum_scatter((adapter_scale * lax.dot_general(picked, cotangent, cont...  160 us
    psum x1, blocking collectives, combine_rows(): return lax.psum(partial_value * keep_mask, 'tensor')  92.6 us
    all_gather x1, blocking collectives, on_device(): lax.all_gather(factor_b, 'dp', axis=0, tiled=True)  80 us
    all_gather x1, waiting for transfers between devices, on_device(): lax.all_gather(factor_a, 'dp', axis=0, tiled=True)  70.8 us
    reduce_scatter x1, waiting for transfers between devices, on_device(): lax.psum_scatter(frozen_out.astype(jnp.bfloat16), 'tensor', scatter_dimen...  43.9 us
  transfers between devices with their start and end apart: 6, of which 5 were waited for; matrix products, arithmetic and copies ran while one was open for 3% of the time, Pallas kernels for 0%

commit v1 on v0

v1 whole, which is shorter than its diff:
```python
import jax
import jax.numpy as jnp
from jax import lax
from jax.experimental import pallas as pl
from jax.experimental.pallas import tpu as pltpu
from jax.sharding import PartitionSpec as P

R = 256
JOBS = 4
BLOCK = 64
NYL, NZ, NX = 4, 8, 4

BF = jnp.bfloat16
F32 = jnp.float32
MESH = pl.DeviceIdType.MESH
NN = (((1,), (0,)), ((), ()))
NT = (((1,), (1,)), ((), ()))
TN = (((0,), (0,)), ((), ()))

adapter_scale = 2.0


def dot(first, second, dims=NN):
    return lax.dot_general(first, second, dims, preferred_element_type=F32)


def loop(count, body, start=1):
    def step(k, carry):
        body(k)
        return carry

    lax.fori_loop(start, start + count, step, 0)


class Sends:
    def __init__(self, sems, base, out, into):
        self.send, self.recv = sems
        self.base, self.out, self.into = base, out, into

    def copy(self, k):
        src, dst, dev = self.out(k)
        return pltpu.make_async_remote_copy(
            src_ref=src,
            dst_ref=dst,
            send_sem=self.send.at[self.base + k],
            recv_sem=self.recv.at[self.base + k],
            device_id=dev,
            device_id_type=MESH,
        )

    def start(self, k):
        self.copy(k).start()

    def landed(self, k):
        src, dst, dev = self.out(k)
        pltpu.make_async_remote_copy(
            src_ref=src,
            dst_ref=self.into(k),
            send_sem=self.send.at[self.base + k],
            recv_sem=self.recv.at[self.base + k],
            device_id=dev,
            device_id_type=MESH,
        ).wait_recv()

    def left(self, k):
        self.copy(k).wait_send()


def kernel(
    hid, w, a, b, cot, lim,
    mixed_o, hg_o, ga_o, gb_o,
    hid_g, w_g, a_g, b_g, cot_g, lim_g, cr,
    part, part_in, tot, yh_out, yh_in, low,
    hg_src, hg_dst, ga_src, ga_dst, gb_src, gb_dst, ml_src, ml_dst,
    fc_src, fc_dst, fx_src, fx_dst, ff_src, ff_dst,
    send_sem, recv_sem,
):
    d = lax.axis_index("dp")
    t = lax.axis_index("tensor")
    yl, z = lax.div(d, 8), lax.rem(d, 8)
    yh, o = lax.div(t, 8), lax.rem(t, 8)
    x, c = lax.div(o, 2), lax.rem(o, 2)

    def yl_at(k):
        return lax.rem(yl + k + 4, 4)

    def z_at(k):
        return lax.rem(z + k + 16, 8)

    def o_at(k):
        return lax.rem(o + k + 8, 8)

    def x_at(k):
        return lax.rem(x + k + 4, 4)

    def yl_peer(k):
        return (yl_at(k) * 8 + z, t)

    def z_peer(k):
        return (yl * 8 + z_at(k), t)

    def o_peer(k):
        return (d, yh * 8 + o_at(k))

    def x_peer(k):
        return (d, yh * 8 + x_at(k) * 2 + c)

    sibling = (d, t + 1 - 2 * c)
    partner = (d, lax.rem(t + 8, 16))

    last_dp = x * 8 + z

    def last_t(xb):
        return lax.div(yl, 2) * 8 + (lax.rem(yl, 2) * 2 + xb) * 2 + c

    def last_here(xb):
        return jnp.logical_and(last_dp == d, last_t(xb) == t)

    first_dp = (2 * yh + lax.div(x, 2)) * 8 + z

    def first_t(h):
        return h * 8 + yl * 2 + c

    def first_here(h):
        return jnp.logical_and(first_dp == d, first_t(h) == t)

    sems = (send_sem, recv_sem)
    bases = [0]

    def family(count, out, into):
        base = bases[0]
        bases[0] += count
        return Sends(sems, base, out, into)

    s_cot = family(4, lambda k: (cot_g.at[yl], cot_g.at[yl], yl_peer(k)), lambda k: cot_g.at[yl_at(-k)])
    s_lim = family(4, lambda k: (lim.at[yl_at(k)], lim_g.at[yl], yl_peer(k)), lambda k: lim_g.at[yl_at(-k)])
    s_hid = family(4, lambda k: (hid_g.at[yl], hid_g.at[yl], yl_peer(k)), lambda k: hid_g.at[yl_at(-k)])
    s_b = family(8, lambda k: (b_g.at[z], b_g.at[z], z_peer(k)), lambda k: b_g.at[z_at(-k)])
    turn = 1 - 2 * c
    rings = []
    for buf in (a_g, w_g):
        right = family(
            4,
            lambda s, buf=buf: (buf.at[z_at(1 - s)], buf.at[z_at(1 - s)], z_peer(1)),
            lambda s, buf=buf: buf.at[z_at(-s)],
        )
        left = family(
            4,
            lambda s, buf=buf: (buf.at[z_at(s - 1)], buf.at[z_at(s - 1)], z_peer(-1)),
            lambda s, buf=buf: buf.at[z_at(s)],
        )
        across = family(
            1,
            lambda s, buf=buf: (buf.at[z_at(-3 * turn)], buf.at[z_at(-3 * turn)], z_peer(turn)),
            lambda s, buf=buf: buf.at[z_at(4)],
        )
        rings.append((right, left, across))

    def ring_start(s):
        for right, left, across in rings:
            if s < 4:
                right.start(s)
                left.start(s)
            else:
                across.start(0)

    def ring_landed(s):
        for right, left, across in rings:
            if s < 4:
                right.landed(s)
                left.landed(s)
            else:
                across.landed(0)

    s_part, s_yh, s_low = [], [], []
    for i in range(2):
        s_part.append(
            family(8, lambda k, i=i: (part.at[i, o_at(k)], part_in.at[i, k], o_peer(k)), lambda k, i=i: part_in.at[i, k])
        )
        s_yh.append(family(1, lambda k, i=i: (yh_out.at[i], yh_in.at[i], partner), lambda k, i=i: yh_in.at[i]))
        s_low.append(
            family(8, lambda k, i=i: (low.at[i, o], low.at[i, o], o_peer(k)), lambda k, i=i: low.at[i, o_at(-k)])
        )

    xb_me = lax.rem(x, 2)
    is_root = lax.div(x, 2) == lax.rem(yl, 2)
    is_native = yh == lax.div(yl, 2)
    native_root = jnp.logical_and(is_root, is_native)
    far_root = jnp.logical_and(is_root, jnp.logical_not(is_native))
    mine = xb_me * 2 + c
    s_cry = family(1, lambda k: (cr.at[mine], cr.at[mine], partner), lambda k: cr.at[mine])
    crx_base = bases[0]
    bases[0] += 4
    crx_recv = bases[0]
    bases[0] += 2

    def crx(k, xb):
        return pltpu.make_async_remote_copy(
            src_ref=cr.at[mine],
            dst_ref=cr.at[xb * 2 + c],
            send_sem=send_sem.at[crx_base + k],
            recv_sem=recv_sem.at[crx_recv + xb],
            device_id=x_peer(k),
            device_id_type=MESH,
        )

    s_crc = family(2, lambda xb: (cr.at[xb * 2 + c], cr.at[xb * 2 + c], sibling), lambda xb: cr.at[xb * 2 + 1 - c])

    hg_base = bases[0]
    bases[0] += 16
    s_hg = [
        Sends(
            sems,
            hg_base + 4 * n,
            lambda k, n=n: (hg_src.at[n, yl_at(k)], hg_dst.at[n, k], yl_peer(k)),
            lambda k, n=n: hg_dst.at[n, k],
        )
        for n in range(4)
    ]
    s_ga = family(8, lambda k: (ga_src.at[z_at(k)], ga_dst.at[k], z_peer(k)), lambda k: ga_dst.at[k])
    s_gb = family(8, lambda k: (gb_src.at[z_at(k)], gb_dst.at[k], z_peer(k)), lambda k: gb_dst.at[k])
    s_ml = family(4, lambda k: (ml_src.at[yl_at(k)], ml_dst.at[k], yl_peer(k)), lambda k: ml_dst.at[k])
    s_fc = family(2, lambda xb: (fc_src.at[xb], fc_dst.at[xb], sibling), lambda xb: fc_dst.at[xb])
    s_fx = family(4, lambda k: (fx_src.at[x_at(k)], fx_dst.at[k], x_peer(k)), lambda k: fx_dst.at[k])
    ff_send = bases[0]
    bases[0] += 2

    def ff(xb, h):
        return pltpu.make_async_remote_copy(
            src_ref=ff_src.at[xb],
            dst_ref=ff_dst.at[h],
            send_sem=send_sem.at[ff_send + xb],
            recv_sem=recv_sem.at[ff_send + h],
            device_id=(last_dp, last_t(xb)),
            device_id_type=MESH,
        )

    cot_g[yl] = cot[...]
    lim_g[yl] = lim[yl]
    b_g[z] = b[...]
    a_g[z] = a[...]
    w_g[z] = w[...]
    hid_g[yl] = hid[...]

    barrier = pltpu.get_barrier_semaphore()

    def greet(dev):
        pl.semaphore_signal(barrier, inc=1, device_id=dev, device_id_type=MESH)

    loop(3, lambda k: greet(yl_peer(k)))
    loop(7, lambda k: greet(z_peer(k)))
    loop(7, lambda k: greet(o_peer(k)))
    greet(partner)
    for xb in range(2):
        @pl.when(jnp.logical_not(last_here(xb)))
        def _(xb=xb):
            greet((last_dp, last_t(xb)))

        @pl.when(jnp.logical_not(first_here(xb)))
        def _(xb=xb):
            greet((first_dp, first_t(xb)))

    own_last = jnp.logical_or(last_here(0), last_here(1)).astype(jnp.int32)
    pl.semaphore_wait(barrier, 22 - 2 * own_last)

    loop(3, s_cot.start)
    loop(3, s_lim.start)
    loop(7, s_b.start)
    ring_start(1)
    loop(3, s_cot.landed)
    loop(3, s_lim.landed)

    @pl.when(native_root)
    def _():
        cr[mine] = cot_g[...].reshape(512, 256)
        s_cry.start(0)
        loop(3, lambda k: crx(k, xb_me).start())

    loop(3, s_hid.start)
    loop(7, s_b.landed)

    def partial(i, value):
        part[i] = value.astype(BF).reshape(8, 64, 256)
        loop(7, s_part[i].start)

    def halfway(i):
        loop(7, s_part[i].landed)
        value = part[i, o].astype(F32)
        for k in range(1, 8):
            value = value + part_in[i, k].astype(F32)
        limit = lim_g[x, pl.ds(pl.multiple_of(c * 8, 8), 8), :][0:1, :]
        limit = jnp.concatenate([limit, limit], axis=1)
        column = lax.broadcasted_iota(jnp.int32, (64, 256), 1).astype(F32)
        value = jnp.where(column < limit, value, 0.0)
        tot[i] = value
        yh_out[i] = value.astype(BF)
        s_yh[i].start(0)

    def whole(i):
        s_yh[i].landed(0)
        low[i, o] = (tot[i] + yh_in[i].astype(F32)).astype(BF)
        loop(7, s_low[i].start)

    factor_b = b_g[...].reshape(256, 256)
    partial(0, dot(cot_g[...].reshape(512, 256), factor_b, NT))

    ring_landed(1)
    ring_start(2)
    halfway(0)

    @pl.when(far_root)
    def _():
        s_cry.landed(0)
        loop(3, lambda k: crx(k, xb_me).start())

    ring_landed(2)
    ring_start(3)
    whole(0)

    for xb in range(2):
        @pl.when(x != lax.rem(yl, 2) * 2 + xb)
        def _(xb=xb):
            crx(1, xb).wait_recv()

        s_crc.start(xb)

    ring_landed(3)
    ring_start(4)

    loop(7, s_low[0].landed)
    for xb in range(2):
        s_crc.landed(xb)
    ring_landed(4)

    def hg_tile(n, send):
        rows = pl.ds(pl.multiple_of(n * 256, 256), 256)
        acc = adapter_scale * dot(low[0].reshape(512, 256), a_g[:, :, rows].reshape(256, 256))
        for j in range(4):
            pair = jnp.concatenate([w_g[2 * j, rows, :], w_g[2 * j + 1, rows, :]], axis=1)
            acc = acc + dot(cr[j], pair, NT)
        hg_src[n] = acc.astype(BF).reshape(4, 128, 256)
        loop(3, send)

    for n in range(4):
        hg_tile(n, s_hg[n].start)

    loop(3, s_hid.landed)
    partial(1, dot(hid_g[...].reshape(512, 1024), a_g[...].reshape(256, 1024), NT))

    def frozen(xb, cc):
        j = xb * 2 + cc
        pair = jnp.concatenate([w_g[2 * j], w_g[2 * j + 1]], axis=1)
        return dot(hid_g[...].reshape(512, 1024), pair)

    for xb in range(2):
        fc_src[xb] = frozen(xb, 1 - c).astype(BF)
        s_fc.start(xb)

    halfway(1)

    def ga_tile(n):
        cols = pl.ds(pl.multiple_of(n * 256, 256), 256)
        term = adapter_scale * dot(low[0].reshape(512, 256), hid_g[:, :, cols].reshape(512, 256), TN)
        ga_src[:, :, cols] = term.astype(BF).reshape(8, 32, 256)

    loop(4, ga_tile, 0)
    loop(7, s_ga.start)
    whole(1)

    for xb in range(2):
        acc = frozen(xb, c)
        s_fc.landed(xb)
        acc = acc + fc_dst[xb].astype(F32)
        fx_src[:, xb] = acc.astype(BF).reshape(4, 128, 256)
    loop(3, s_fx.start)

    loop(7, s_low[1].landed)
    ml_src[...] = (adapter_scale * dot(low[1].reshape(512, 256), factor_b)).astype(BF).reshape(4, 128, 256)
    loop(3, s_ml.start)
    gb_src[...] = (
        adapter_scale * dot(low[1].reshape(512, 256), cot_g[...].reshape(512, 256), TN)
    ).astype(BF).reshape(8, 32, 256)
    loop(7, s_gb.start)

    loop(3, s_fx.landed)
    value = fx_src[x].astype(F32)
    for k in range(1, 4):
        value = value + fx_dst[k].astype(F32)
    ff_src[...] = value.astype(BF)
    for xb in range(2):
        @pl.when(last_here(xb))
        def _(xb=xb):
            ff_dst[yh] = ff_src[xb]

        @pl.when(jnp.logical_not(last_here(xb)))
        def _(xb=xb):
            ff(xb, yh).start()

    for n in range(4):
        loop(3, s_hg[n].landed)
        value = hg_src[n, yl].astype(F32)
        for k in range(1, 4):
            value = value + hg_dst[n, k].astype(F32)
        hg_o[:, 256 * n : 256 * (n + 1)] = value.astype(BF)

    loop(7, s_ga.landed)
    value = ga_src[z].astype(F32)
    for k in range(1, 8):
        value = value + ga_dst[k].astype(F32)
    ga_o[...] = value.astype(BF)

    loop(7, s_gb.landed)
    value = gb_src[z].astype(F32)
    for k in range(1, 8):
        value = value + gb_dst[k].astype(F32)
    gb_o[...] = value.astype(BF)

    loop(3, s_ml.landed)
    for h in range(2):
        @pl.when(jnp.logical_not(first_here(h)))
        def _(h=h):
            ff(0, h).wait_recv()

    value = ff_dst[0].astype(F32) + ff_dst[1].astype(F32) + ml_src[yl].astype(F32)
    for k in range(1, 4):
        value = value + ml_dst[k].astype(F32)
    mixed_o[...] = value.astype(BF)

    for family_of in (s_cot, s_lim, s_hid, s_ml, s_fx, *s_hg):
        loop(3, family_of.left)
    for family_of in (s_b, *s_part, *s_low, s_ga, s_gb):
        loop(7, family_of.left)
    for right, left, across in rings:
        loop(3, right.left)
        loop(3, left.left)
        across.left(0)
    for family_of in s_yh:
        family_of.left(0)
    for xb in range(2):
        s_crc.left(xb)
        s_fc.left(xb)

        @pl.when(jnp.logical_not(last_here(xb)))
        def _(xb=xb):
            ff(xb, yh).wait_send()

    @pl.when(native_root)
    def _():
        s_cry.left(0)

    @pl.when(is_root)
    def _():
        loop(3, lambda k: crx(k, xb_me).wait_send())


SEMS = 192


def on_device(hidden, down_weight, factor_a, factor_b, cotangent, block_job, ranks):
    jobs = jnp.arange(JOBS, dtype=jnp.int32)
    limit = jnp.where(block_job[:, 0][None, :] == jobs[:, None], ranks[:, None], 0)
    limit = jnp.repeat(limit, 8, axis=1).astype(F32)
    limit = jnp.broadcast_to(limit[:, :, None], (JOBS, 16, 128))

    def vmem(*shape, dtype=BF):
        return pltpu.VMEM(shape, dtype)

    shapes = ((128, 256), (128, 1024), (32, 1024), (32, 256))
    return pl.pallas_call(
        kernel,
        out_shape=tuple(jax.ShapeDtypeStruct(s, BF) for s in shapes),
        in_specs=[pl.BlockSpec(memory_space=pltpu.VMEM)] * 6,
        out_specs=tuple(pl.BlockSpec(memory_space=pltpu.VMEM) for s in shapes),
        scratch_shapes=[
            vmem(4, 128, 1024), vmem(8, 1024, 128), vmem(8, 32, 1024), vmem(8, 32, 256),
            vmem(4, 128, 256), vmem(4, 16, 128, dtype=F32), vmem(4, 512, 256),
            vmem(2, 8, 64, 256), vmem(2, 8, 64, 256), vmem(2, 64, 256, dtype=F32),
            vmem(2, 64, 256), vmem(2, 64, 256), vmem(2, 8, 64, 256),
            vmem(4, 4, 128, 256), vmem(4, 4, 128, 256), vmem(8, 32, 1024), vmem(8, 32, 1024),
            vmem(8, 32, 256), vmem(8, 32, 256), vmem(4, 128, 256), vmem(4, 128, 256),
            vmem(2, 512, 256), vmem(2, 512, 256), vmem(4, 2, 128, 256), vmem(4, 2, 128, 256),
            vmem(2, 128, 256), vmem(2, 128, 256),
            pltpu.SemaphoreType.DMA((SEMS,)), pltpu.SemaphoreType.DMA((SEMS,)),
        ],
        compiler_params=pltpu.CompilerParams(
            collective_id=0, has_side_effects=True, vmem_limit_bytes=48 * 1024 * 1024
        ),
        cost_estimate=pl.CostEstimate(flops=3_000_000_000, bytes_accessed=4_000_000, transcendentals=0),
    )(hidden, down_weight, factor_a, factor_b, cotangent, limit)


def solution(mesh):
    in_specs = (
        P("dp", "tensor"),
        P("tensor", "dp"),
        P("dp", "tensor"),
        P("dp", "tensor"),
        P("dp", "tensor"),
        P("dp", None),
        P(),
    )
    out_specs = (P("dp", "tensor"), P("dp", "tensor"), P("dp", "tensor"), P("dp", "tensor"))
    return jax.shard_map(
        on_device, mesh=mesh, in_specs=in_specs, out_specs=out_specs, check_vma=False
    )
```

time: 826 us -> 113 us (0.14)
  the two profiles are of different devices: /device:TPU:6 before, /device:TPU:1 now
where the time goes in v1:
time: 113 us; the launch traced here: 112 us
  Pallas kernels  104 us (92%)
  local copies, waits for them, and re-layouts  7.68 us (7%)
    pallas_call x1, Pallas kernels, on_device(): pl.pallas_call(kernel, out_shape=tuple((jax.ShapeDtypeStruct(s, BF) for s...  104 us
    unnamed x18, local copies, waits for them, and re-layouts  7.45 us

profile of v1, /device:TPU:1, one launch (start us, length us, event | category | flops | bytes accessed | tf_op | source)
XLA Modules:
  0.0 112.3 jit_solution(2912912818811120585)
XLA Ops:
  0.6 0.0 copy-start.5
  0.6 0.0 copy-start.6
  0.7 0.6 copy-done.5
  1.3 0.0 copy-done.6
  1.3 0.1 select_convert_fusion
  1.4 0.1 broadcast_in_dim.25
  1.4 0.1 convert_element_type.12
  1.5 0.0 copy-start.4
  1.5 0.1 broadcast_in_dim.26.lim
  1.6 0.6 copy-done.4
  2.3 0.0 copy-start
  2.3 0.9 copy-done
  3.2 0.0 copy-start.1
  3.2 0.9 copy-done.1
  4.2 0.0 copy-start.2
  4.2 0.8 copy-done.2
  5.0 0.0 copy-start.3
  5.0 0.8 copy-done.3
  5.8 103.9 %shard_map.102 = (bf16[128,256]{1,0:T(8,128)(2,1)S(1)}, bf16[128,1024]{1,0:T(8,128)(2,1)S(1)}, bf16[32,1024]{1,0:T(8,128)(2,1)S(1)}, bf16[32,256]{1,0:T(8,128)(2,1)S(1)}) custom-call(bf16[128,1024]{1,0:T(8,128)(2,1)S(1)} %copy-done, bf16[1024,128]{1,0:T(8,128)(2,1)S(1)} %copy-done.1, bf16[32,1024]{1,0:T(8,128)(2,1)S(1)} %copy-done.2, ...), custom_call_target="tpu_custom_call" | custom-call | flops 3000000000 | bytes 4000000 | tf_op jit(solution)/shard_map/pallas_call | solution.py:469
  109.7 0.6 copy.15
  110.3 0.7 copy.16
  111.0 0.6 copy.17
  111.7 0.6 copy.18
Async XLA Ops:
  0.6 0.7 copy-start.5
  0.6 0.7 copy-start.6
  1.5 0.7 copy-start.4
  2.3 0.9 copy-start
  3.2 0.9 copy-start.1
  4.2 0.8 copy-start.2
  5.0 0.8 copy-start.3

commit v2 on v1

--- a/solution.py
+++ b/solution.py
@@ -67,13 +67,13 @@
 
 
 def kernel(
-    hid, w, a, b, cot, lim,
+    hid, w, a, b, cot, block_job, ranks,
     mixed_o, hg_o, ga_o, gb_o,
-    hid_g, w_g, a_g, b_g, cot_g, lim_g, cr,
+    hid_g, w_g, a_g, b_g, cot_g, lim, lim_g, cr,
     part, part_in, tot, yh_out, yh_in, low,
     hg_src, hg_dst, ga_src, ga_dst, gb_src, gb_dst, ml_src, ml_dst,
     fc_src, fc_dst, fx_src, fx_dst, ff_src, ff_dst,
-    send_sem, recv_sem,
+    own_sem, send_sem, recv_sem,
 ):
     d = lax.axis_index("dp")
     t = lax.axis_index("tensor")
@@ -134,43 +134,52 @@
 
     s_cot = family(4, lambda k: (cot_g.at[yl], cot_g.at[yl], yl_peer(k)), lambda k: cot_g.at[yl_at(-k)])
     s_lim = family(4, lambda k: (lim.at[yl_at(k)], lim_g.at[yl], yl_peer(k)), lambda k: lim_g.at[yl_at(-k)])
-    s_hid = family(4, lambda k: (hid_g.at[yl], hid_g.at[yl], yl_peer(k)), lambda k: hid_g.at[yl_at(-k)])
+    s_hid = [
+        family(
+            4,
+            lambda k, h=h: (hid_g.at[yl, h], hid_g.at[yl, h], yl_peer(k)),
+            lambda k, h=h: hid_g.at[yl_at(-k), h],
+        )
+        for h in (pl.ds(0, 64), pl.ds(64, 64))
+    ]
     s_b = family(8, lambda k: (b_g.at[z], b_g.at[z], z_peer(k)), lambda k: b_g.at[z_at(-k)])
     turn = 1 - 2 * c
     rings = []
-    for buf in (a_g, w_g):
+    for at in (
+        lambda slot: a_g.at[slot],
+        lambda slot: w_g.at[slot, pl.ds(0, 512)],
+        lambda slot: w_g.at[slot, pl.ds(512, 512)],
+    ):
         right = family(
             4,
-            lambda s, buf=buf: (buf.at[z_at(1 - s)], buf.at[z_at(1 - s)], z_peer(1)),
-            lambda s, buf=buf: buf.at[z_at(-s)],
+            lambda s, at=at: (at(z_at(1 - s)), at(z_at(1 - s)), z_peer(1)),
+            lambda s, at=at: at(z_at(-s)),
         )
         left = family(
             4,
-            lambda s, buf=buf: (buf.at[z_at(s - 1)], buf.at[z_at(s - 1)], z_peer(-1)),
-            lambda s, buf=buf: buf.at[z_at(s)],
+            lambda s, at=at: (at(z_at(s - 1)), at(z_at(s - 1)), z_peer(-1)),
+            lambda s, at=at: at(z_at(s)),
         )
         across = family(
             1,
-            lambda s, buf=buf: (buf.at[z_at(-3 * turn)], buf.at[z_at(-3 * turn)], z_peer(turn)),
-            lambda s, buf=buf: buf.at[z_at(4)],
+            lambda s, at=at: (at(z_at(-3 * turn)), at(z_at(-3 * turn)), z_peer(turn)),
+            lambda s, at=at: at(z_at(4)),
         )
         rings.append((right, left, across))
 
-    def ring_start(s):
+    def ring_pass(s):
         for right, left, across in rings:
-            if s < 4:
-                right.start(s)
-                left.start(s)
+            if s == 4:
+                across.landed(0)
+                continue
+            if s > 0:
+                right.landed(s)
+                left.landed(s)
+            if s < 3:
+                right.start(s + 1)
+                left.start(s + 1)
             else:
                 across.start(0)
-
-    def ring_landed(s):
-        for right, left, across in rings:
-            if s < 4:
-                right.landed(s)
-                left.landed(s)
-            else:
-                across.landed(0)
 
     s_part, s_yh, s_low = [], [], []
     for i in range(2):
@@ -188,7 +197,20 @@
     native_root = jnp.logical_and(is_root, is_native)
     far_root = jnp.logical_and(is_root, jnp.logical_not(is_native))
     mine = xb_me * 2 + c
-    s_cry = family(1, lambda k: (cr.at[mine], cr.at[mine], partner), lambda k: cr.at[mine])
+    far_row = (2 * yh + lax.div(x, 2)) * 8 + z
+    cry_base = bases[0]
+    bases[0] += 4
+
+    def cry(row):
+        return pltpu.make_async_remote_copy(
+            src_ref=cot_g.at[yl],
+            dst_ref=cr.at[mine, row],
+            send_sem=send_sem.at[cry_base],
+            recv_sem=recv_sem.at[cry_base + row],
+            device_id=(far_row, lax.rem(t + 8, 16)),
+            device_id_type=MESH,
+        )
+
     crx_base = bases[0]
     bases[0] += 4
     crx_recv = bases[0]
@@ -235,12 +257,16 @@
             device_id_type=MESH,
         )
 
-    cot_g[yl] = cot[...]
-    lim_g[yl] = lim[yl]
-    b_g[z] = b[...]
-    a_g[z] = a[...]
-    w_g[z] = w[...]
-    hid_g[yl] = hid[...]
+    assert bases[0] <= SEMS
+
+    own = [
+        pltpu.make_async_copy(src, dst, own_sem.at[i])
+        for i, (src, dst) in enumerate(
+            ((cot, cot_g.at[yl]), (b, b_g.at[z]), (a, a_g.at[z]), (w, w_g.at[z]), (hid, hid_g.at[yl]))
+        )
+    ]
+    for copy in own:
+        copy.start()
 
     barrier = pltpu.get_barrier_semaphore()
 
@@ -261,22 +287,35 @@
             greet((first_dp, first_t(xb)))
 
     own_last = jnp.logical_or(last_here(0), last_here(1)).astype(jnp.int32)
-    pl.semaphore_wait(barrier, 22 - 2 * own_last)
+    greet((far_row, lax.rem(t + 8, 16)))
+
+    @pl.when(far_root)
+    def _():
+        loop(4, lambda row: greet((row * 8 + z, lax.rem(t + 8, 16))), 0)
+
+    row = lax.broadcasted_iota(jnp.int32, (16, 128), 0)
+    job = jnp.where(row < 8, block_job[0, 0], block_job[1, 0])
+    for j in range(JOBS):
+        lim[j] = jnp.where(job == j, ranks[j], 0).astype(F32)
+    lim_g[yl] = lim[yl]
+
+    for copy in own:
+        copy.wait()
+    pl.semaphore_wait(barrier, 23 - 2 * own_last + 4 * far_root.astype(jnp.int32))
 
     loop(3, s_cot.start)
+    cry(yl).start()
     loop(3, s_lim.start)
+    ring_pass(0)
     loop(7, s_b.start)
-    ring_start(1)
     loop(3, s_cot.landed)
-    loop(3, s_lim.landed)
 
     @pl.when(native_root)
     def _():
-        cr[mine] = cot_g[...].reshape(512, 256)
-        s_cry.start(0)
+        cr[mine] = cot_g[...]
         loop(3, lambda k: crx(k, xb_me).start())
 
-    loop(3, s_hid.start)
+    loop(3, s_hid[0].start)
     loop(7, s_b.landed)
 
     def partial(i, value):
@@ -304,18 +343,19 @@
     factor_b = b_g[...].reshape(256, 256)
     partial(0, dot(cot_g[...].reshape(512, 256), factor_b, NT))
 
-    ring_landed(1)
-    ring_start(2)
-    halfway(0)
-
     @pl.when(far_root)
     def _():
-        s_cry.landed(0)
+        for row in range(4):
+            cry(row).wait_recv()
         loop(3, lambda k: crx(k, xb_me).start())
 
-    ring_landed(2)
-    ring_start(3)
+    ring_pass(1)
+    loop(3, s_lim.landed)
+    halfway(0)
+    loop(3, s_hid[1].start)
+    ring_pass(2)
     whole(0)
+    ring_pass(3)
 
     for xb in range(2):
         @pl.when(x != lax.rem(yl, 2) * 2 + xb)
@@ -324,55 +364,52 @@
 
         s_crc.start(xb)
 
-    ring_landed(3)
-    ring_start(4)
+    for half in s_hid:
+        loop(3, half.landed)
+    ring_pass(4)
+    partial(1, dot(hid_g[...].reshape(512, 1024), a_g[...].reshape(256, 1024), NT))
 
     loop(7, s_low[0].landed)
     for xb in range(2):
         s_crc.landed(xb)
-    ring_landed(4)
-
-    def hg_tile(n, send):
-        rows = pl.ds(pl.multiple_of(n * 256, 256), 256)
+
+    def hg_tile(n):
+        rows = slice(256 * n, 256 * (n + 1))
         acc = adapter_scale * dot(low[0].reshape(512, 256), a_g[:, :, rows].reshape(256, 256))
         for j in range(4):
             pair = jnp.concatenate([w_g[2 * j, rows, :], w_g[2 * j + 1, rows, :]], axis=1)
-            acc = acc + dot(cr[j], pair, NT)
+            acc = acc + dot(cr[j].reshape(512, 256), pair, NT)
         hg_src[n] = acc.astype(BF).reshape(4, 128, 256)
-        loop(3, send)
-
-    for n in range(4):
-        hg_tile(n, s_hg[n].start)
-
-    loop(3, s_hid.landed)
-    partial(1, dot(hid_g[...].reshape(512, 1024), a_g[...].reshape(256, 1024), NT))
+        loop(3, s_hg[n].start)
 
     def frozen(xb, cc):
         j = xb * 2 + cc
         pair = jnp.concatenate([w_g[2 * j], w_g[2 * j + 1]], axis=1)
         return dot(hid_g[...].reshape(512, 1024), pair)
 
+    hg_tile(0)
+    hg_tile(1)
     for xb in range(2):
         fc_src[xb] = frozen(xb, 1 - c).astype(BF)
         s_fc.start(xb)
 
     halfway(1)
-
-    def ga_tile(n):
-        cols = pl.ds(pl.multiple_of(n * 256, 256), 256)
-        term = adapter_scale * dot(low[0].reshape(512, 256), hid_g[:, :, cols].reshape(512, 256), TN)
-        ga_src[:, :, cols] = term.astype(BF).reshape(8, 32, 256)
-
-    loop(4, ga_tile, 0)
-    loop(7, s_ga.start)
-    whole(1)
-
+    hg_tile(2)
     for xb in range(2):
         acc = frozen(xb, c)
         s_fc.landed(xb)
         acc = acc + fc_dst[xb].astype(F32)
         fx_src[:, xb] = acc.astype(BF).reshape(4, 128, 256)
     loop(3, s_fx.start)
+
+    whole(1)
+    hg_tile(3)
+
+    for n in range(4):
+        cols = slice(256 * n, 256 * (n + 1))
+        term = adapter_scale * dot(low[0].reshape(512, 256), hid_g[:, :, cols].reshape(512, 256), TN)
+        ga_src[:, :, cols] = term.astype(BF).reshape(8, 32, 256)
+    loop(7, s_ga.start)
 
     loop(7, s_low[1].landed)
     ml_src[...] = (adapter_scale * dot(low[1].reshape(512, 256), factor_b)).astype(BF).reshape(4, 128, 256)
@@ -426,7 +463,7 @@
         value = value + ml_dst[k].astype(F32)
     mixed_o[...] = value.astype(BF)
 
-    for family_of in (s_cot, s_lim, s_hid, s_ml, s_fx, *s_hg):
+    for family_of in (s_cot, s_lim, *s_hid, s_ml, s_fx, *s_hg):
         loop(3, family_of.left)
     for family_of in (s_b, *s_part, *s_low, s_ga, s_gb):
         loop(7, family_of.left)
@@ -444,24 +481,17 @@
         def _(xb=xb):
             ff(xb, yh).wait_send()
 
-    @pl.when(native_root)
-    def _():
-        s_cry.left(0)
+    cry(yl).wait_send()
 
     @pl.when(is_root)
     def _():
         loop(3, lambda k: crx(k, xb_me).wait_send())
 
 
-SEMS = 192
+SEMS = 160
 
 
 def on_device(hidden, down_weight, factor_a, factor_b, cotangent, block_job, ranks):
-    jobs = jnp.arange(JOBS, dtype=jnp.int32)
-    limit = jnp.where(block_job[:, 0][None, :] == jobs[:, None], ranks[:, None], 0)
-    limit = jnp.repeat(limit, 8, axis=1).astype(F32)
-    limit = jnp.broadcast_to(limit[:, :, None], (JOBS, 16, 128))
-
     def vmem(*shape, dtype=BF):
         return pltpu.VMEM(shape, dtype)
 
@@ -469,24 +499,24 @@
     return pl.pallas_call(
         kernel,
         out_shape=tuple(jax.ShapeDtypeStruct(s, BF) for s in shapes),
-        in_specs=[pl.BlockSpec(memory_space=pltpu.VMEM)] * 6,
+        in_specs=[pl.BlockSpec(memory_space=pltpu.HBM)] * 5 + [pl.BlockSpec(memory_space=pltpu.SMEM)] * 2,
         out_specs=tuple(pl.BlockSpec(memory_space=pltpu.VMEM) for s in shapes),
         scratch_shapes=[
             vmem(4, 128, 1024), vmem(8, 1024, 128), vmem(8, 32, 1024), vmem(8, 32, 256),
-            vmem(4, 128, 256), vmem(4, 16, 128, dtype=F32), vmem(4, 512, 256),
+            vmem(4, 128, 256), vmem(4, 16, 128, dtype=F32), vmem(4, 16, 128, dtype=F32), vmem(4, 4, 128, 256),
             vmem(2, 8, 64, 256), vmem(2, 8, 64, 256), vmem(2, 64, 256, dtype=F32),
             vmem(2, 64, 256), vmem(2, 64, 256), vmem(2, 8, 64, 256),
             vmem(4, 4, 128, 256), vmem(4, 4, 128, 256), vmem(8, 32, 1024), vmem(8, 32, 1024),
             vmem(8, 32, 256), vmem(8, 32, 256), vmem(4, 128, 256), vmem(4, 128, 256),
             vmem(2, 512, 256), vmem(2, 512, 256), vmem(4, 2, 128, 256), vmem(4, 2, 128, 256),
             vmem(2, 128, 256), vmem(2, 128, 256),
-            pltpu.SemaphoreType.DMA((SEMS,)), pltpu.SemaphoreType.DMA((SEMS,)),
+            pltpu.SemaphoreType.DMA((5,)), pltpu.SemaphoreType.DMA((SEMS,)), pltpu.SemaphoreType.DMA((SEMS,)),
         ],
         compiler_params=pltpu.CompilerParams(
-            collective_id=0, has_side_effects=True, vmem_limit_bytes=48 * 1024 * 1024
+            collective_id=0, has_side_effects=True, vmem_limit_bytes=54528 * 1024
         ),
         cost_estimate=pl.CostEstimate(flops=3_000_000_000, bytes_accessed=4_000_000, transcendentals=0),
-    )(hidden, down_weight, factor_a, factor_b, cotangent, limit)
+    )(hidden, down_weight, factor_a, factor_b, cotangent, block_job, ranks)
 
 
 def solution(mesh):

time: 113 us -> 99.3 us (0.88)
  the two profiles are of different devices: /device:TPU:1 before, /device:TPU:6 now
where the time goes in v2:
time: 99.3 us; the launch traced here: 99 us
  Pallas kernels  92.6 us (93%)
  local copies, waits for them, and re-layouts  5.71 us (6%)
    pallas_call x1, Pallas kernels, on_device(): pl.pallas_call(kernel, out_shape=tuple((jax.ShapeDtypeStruct(s, BF) for s...  92.6 us
    unnamed x13, local copies, waits for them, and re-layouts  5.71 us

profile of v2, /device:TPU:6, one launch (start us, length us, event | category | flops | bytes accessed | tf_op | source)
XLA Modules:
  0.0 99.0 jit_solution(6217568091592716063)
XLA Ops:
  0.6 0.0 copy-start.3
  0.6 0.7 copy.11.block_job
  1.4 0.0 copy-done.3
  1.4 0.0 copy-start
  1.4 0.8 copy-done
  2.2 0.0 copy-start.1
  2.2 0.8 copy-done.1
  3.1 0.0 copy-start.2
  3.1 0.7 copy-done.2
  3.8 92.6 %shard_map.102 = (bf16[128,256]{1,0:T(8,128)(2,1)S(1)}, bf16[128,1024]{1,0:T(8,128)(2,1)S(1)}, bf16[32,1024]{1,0:T(8,128)(2,1)S(1)}, bf16[32,256]{1,0:T(8,128)(2,1)S(1)}) custom-call(bf16[128,1024]{1,0:T(8,128)(2,1)} %hid.1, bf16[1024,128]{1,0:T(8,128)(2,1)} %w.1, bf16[32,1024]{1,0:T(8,128)(2,1)S(1)} %copy-done, bf16[32,256]{1,0:T(8,128)(2,1)S(1)} %copy-done.2, ...), custom_call_target="tpu_custom_call" | custom-call | flops 3000000000 | bytes 4000000 | tf_op jit(solution)/shard_map/pallas_call | solution.py:499
  96.4 0.6 copy.16
  97.1 0.7 copy.17
  97.8 0.6 copy.18
  98.4 0.6 copy.19
Async XLA Ops:
  0.6 0.8 copy-start.3
  1.4 0.8 copy-start
  2.2 0.8 copy-start.1
  3.1 0.7 copy-start.2

commit v3 on v2

--- a/solution.py
+++ b/solution.py
@@ -71,7 +71,7 @@
     mixed_o, hg_o, ga_o, gb_o,
     hid_g, w_g, a_g, b_g, cot_g, lim, lim_g, cr,
     part, part_in, tot, yh_out, yh_in, low,
-    hg_src, hg_dst, ga_src, ga_dst, gb_src, gb_dst, ml_src, ml_dst,
+    hg_src, hg_far, hg_sum, hg_dst, ga_src, ga_dst, gb_src, gb_dst, ml_src, ml_dst,
     fc_src, fc_dst, fx_src, fx_dst, ff_src, ff_dst,
     own_sem, send_sem, recv_sem,
 ):
@@ -191,12 +191,14 @@
             family(8, lambda k, i=i: (low.at[i, o], low.at[i, o], o_peer(k)), lambda k, i=i: low.at[i, o_at(-k)])
         )
 
-    xb_me = lax.rem(x, 2)
+    odd = lax.rem(x, 2)
     is_root = lax.div(x, 2) == lax.rem(yl, 2)
     is_native = yh == lax.div(yl, 2)
     native_root = jnp.logical_and(is_root, is_native)
     far_root = jnp.logical_and(is_root, jnp.logical_not(is_native))
-    mine = xb_me * 2 + c
+    root_piece = odd * 2 + c
+    nearer = jnp.where(is_root, odd, 1 - odd)
+    piece, other_piece = nearer * 2 + c, (1 - nearer) * 2 + c
     far_row = (2 * yh + lax.div(x, 2)) * 8 + z
     cry_base = bases[0]
     bases[0] += 4
@@ -204,41 +206,49 @@
     def cry(row):
         return pltpu.make_async_remote_copy(
             src_ref=cot_g.at[yl],
-            dst_ref=cr.at[mine, row],
+            dst_ref=cr.at[root_piece, row],
             send_sem=send_sem.at[cry_base],
             recv_sem=recv_sem.at[cry_base + row],
             device_id=(far_row, lax.rem(t + 8, 16)),
             device_id_type=MESH,
         )
 
-    crx_base = bases[0]
-    bases[0] += 4
-    crx_recv = bases[0]
-    bases[0] += 2
-
-    def crx(k, xb):
+    s_out = family(
+        4, lambda row: (cr.at[piece, row], cr.at[piece, row], x_peer(2 * odd - 1)), lambda row: cr.at[piece, row]
+    )
+    s_over = family(
+        4, lambda row: (cr.at[piece, row], cr.at[piece, row], x_peer(1 - 2 * odd)), lambda row: cr.at[other_piece, row]
+    )
+    s_crc = family(2, lambda xb: (cr.at[xb * 2 + c], cr.at[xb * 2 + c], sibling), lambda xb: cr.at[xb * 2 + 1 - c])
+
+    side = lax.div(yl, 2)
+    mate_row = yl + 1 - 2 * lax.rem(yl, 2)
+    mate = (mate_row * 8 + z, t)
+    at_edge = lax.rem(yl, 2) == side
+    at_middle = jnp.logical_not(at_edge)
+
+    def other_row(q):
+        return 2 - side if q == 0 else 3 * (1 - side)
+
+    s_hg_near = family(4, lambda n: (hg_src.at[n, mate_row], hg_dst.at[n, 0], mate), lambda n: hg_dst.at[n, 0])
+    s_hg_far = []
+    for q in range(2):
+        s_hg_far.append(
+            family(4, lambda n, q=q: (hg_src.at[n, other_row(q)], hg_far.at[n, q], mate), lambda n, q=q: hg_far.at[n, q])
+        )
+    hg_sum_send = bases[0]
+    bases[0] += 8
+
+    def hg_total(n, q):
         return pltpu.make_async_remote_copy(
-            src_ref=cr.at[mine],
-            dst_ref=cr.at[xb * 2 + c],
-            send_sem=send_sem.at[crx_base + k],
-            recv_sem=recv_sem.at[crx_recv + xb],
-            device_id=x_peer(k),
+            src_ref=hg_sum.at[n, q],
+            dst_ref=hg_dst.at[n, 1],
+            send_sem=send_sem.at[hg_sum_send + 4 * q + n],
+            recv_sem=recv_sem.at[hg_sum_send + n],
+            device_id=(other_row(q) * 8 + z, t),
             device_id_type=MESH,
         )
 
-    s_crc = family(2, lambda xb: (cr.at[xb * 2 + c], cr.at[xb * 2 + c], sibling), lambda xb: cr.at[xb * 2 + 1 - c])
-
-    hg_base = bases[0]
-    bases[0] += 16
-    s_hg = [
-        Sends(
-            sems,
-            hg_base + 4 * n,
-            lambda k, n=n: (hg_src.at[n, yl_at(k)], hg_dst.at[n, k], yl_peer(k)),
-            lambda k, n=n: hg_dst.at[n, k],
-        )
-        for n in range(4)
-    ]
     s_ga = family(8, lambda k: (ga_src.at[z_at(k)], ga_dst.at[k], z_peer(k)), lambda k: ga_dst.at[k])
     s_gb = family(8, lambda k: (gb_src.at[z_at(k)], gb_dst.at[k], z_peer(k)), lambda k: gb_dst.at[k])
     s_ml = family(4, lambda k: (ml_src.at[yl_at(k)], ml_dst.at[k], yl_peer(k)), lambda k: ml_dst.at[k])
@@ -312,8 +322,10 @@
 
     @pl.when(native_root)
     def _():
-        cr[mine] = cot_g[...]
-        loop(3, lambda k: crx(k, xb_me).start())
+        cr[piece] = cot_g[...]
+        for row in range(4):
+            s_out.start(row)
+            s_over.start(row)
 
     loop(3, s_hid[0].start)
     loop(7, s_b.landed)
@@ -347,22 +359,25 @@
     def _():
         for row in range(4):
             cry(row).wait_recv()
-        loop(3, lambda k: crx(k, xb_me).start())
+            s_out.start(row)
+            s_over.start(row)
 
     ring_pass(1)
     loop(3, s_lim.landed)
     halfway(0)
     loop(3, s_hid[1].start)
+    @pl.when(jnp.logical_not(is_root))
+    def _():
+        for row in range(4):
+            s_out.landed(row)
+            s_over.start(row)
+
     ring_pass(2)
     whole(0)
+    s_crc.start(nearer)
     ring_pass(3)
-
-    for xb in range(2):
-        @pl.when(x != lax.rem(yl, 2) * 2 + xb)
-        def _(xb=xb):
-            crx(1, xb).wait_recv()
-
-        s_crc.start(xb)
+    loop(4, s_over.landed, 0)
+    s_crc.start(1 - nearer)
 
     for half in s_hid:
         loop(3, half.landed)
@@ -380,7 +395,22 @@
             pair = jnp.concatenate([w_g[2 * j, rows, :], w_g[2 * j + 1, rows, :]], axis=1)
             acc = acc + dot(cr[j].reshape(512, 256), pair, NT)
         hg_src[n] = acc.astype(BF).reshape(4, 128, 256)
-        loop(3, s_hg[n].start)
+
+        @pl.when(at_edge)
+        def _():
+            s_hg_far[1].start(n)
+            s_hg_far[0].start(n)
+
+        s_hg_near.start(n)
+
+    def hg_middle(n):
+        @pl.when(at_middle)
+        def _():
+            for q in (1, 0):
+                s_hg_far[q].landed(n)
+                own_term = hg_src[n, other_row(q)].astype(F32)
+                hg_sum[n, q] = (own_term + hg_far[n, q].astype(F32)).astype(BF)
+                hg_total(n, q).start()
 
     def frozen(xb, cc):
         j = xb * 2 + cc
@@ -393,7 +423,14 @@
         fc_src[xb] = frozen(xb, 1 - c).astype(BF)
         s_fc.start(xb)
 
+    for n in range(4):
+        cols = slice(256 * n, 256 * (n + 1))
+        term = adapter_scale * dot(low[0].reshape(512, 256), hid_g[:, :, cols].reshape(512, 256), TN)
+        ga_src[:, :, cols] = term.astype(BF).reshape(8, 32, 256)
+    loop(7, s_ga.start)
+
     halfway(1)
+    hg_middle(0)
     hg_tile(2)
     for xb in range(2):
         acc = frozen(xb, c)
@@ -402,23 +439,10 @@
         fx_src[:, xb] = acc.astype(BF).reshape(4, 128, 256)
     loop(3, s_fx.start)
 
+    hg_middle(1)
+    hg_tile(3)
     whole(1)
-    hg_tile(3)
-
-    for n in range(4):
-        cols = slice(256 * n, 256 * (n + 1))
-        term = adapter_scale * dot(low[0].reshape(512, 256), hid_g[:, :, cols].reshape(512, 256), TN)
-        ga_src[:, :, cols] = term.astype(BF).reshape(8, 32, 256)
-    loop(7, s_ga.start)
-
-    loop(7, s_low[1].landed)
-    ml_src[...] = (adapter_scale * dot(low[1].reshape(512, 256), factor_b)).astype(BF).reshape(4, 128, 256)
-    loop(3, s_ml.start)
-    gb_src[...] = (
-        adapter_scale * dot(low[1].reshape(512, 256), cot_g[...].reshape(512, 256), TN)
-    ).astype(BF).reshape(8, 32, 256)
-    loop(7, s_gb.start)
-
+    hg_middle(2)
     loop(3, s_fx.landed)
     value = fx_src[x].astype(F32)
     for k in range(1, 4):
@@ -433,11 +457,20 @@
         def _(xb=xb):
             ff(xb, yh).start()
 
+    hg_middle(3)
+    loop(7, s_low[1].landed)
+    gb_src[...] = (
+        adapter_scale * dot(low[1].reshape(512, 256), cot_g[...].reshape(512, 256), TN)
+    ).astype(BF).reshape(8, 32, 256)
+    loop(7, s_gb.start)
+
+    ml_src[...] = (adapter_scale * dot(low[1].reshape(512, 256), factor_b)).astype(BF).reshape(4, 128, 256)
+    loop(3, s_ml.start)
+
     for n in range(4):
-        loop(3, s_hg[n].landed)
-        value = hg_src[n, yl].astype(F32)
-        for k in range(1, 4):
-            value = value + hg_dst[n, k].astype(F32)
+        s_hg_near.landed(n)
+        hg_total(n, 0).wait_recv()
+        value = hg_src[n, yl].astype(F32) + hg_dst[n, 0].astype(F32) + hg_dst[n, 1].astype(F32)
         hg_o[:, 256 * n : 256 * (n + 1)] = value.astype(BF)
 
     loop(7, s_ga.landed)
@@ -463,7 +496,7 @@
         value = value + ml_dst[k].astype(F32)
     mixed_o[...] = value.astype(BF)
 
-    for family_of in (s_cot, s_lim, *s_hid, s_ml, s_fx, *s_hg):
+    for family_of in (s_cot, s_lim, *s_hid, s_ml, s_fx):
         loop(3, family_of.left)
     for family_of in (s_b, *s_part, *s_low, s_ga, s_gb):
         loop(7, family_of.left)
@@ -482,10 +515,24 @@
             ff(xb, yh).wait_send()
 
     cry(yl).wait_send()
+    loop(4, s_hg_near.left, 0)
+
+    @pl.when(at_edge)
+    def _():
+        for q in range(2):
+            loop(4, s_hg_far[q].left, 0)
+
+    @pl.when(at_middle)
+    def _():
+        for n in range(4):
+            for q in range(2):
+                hg_total(n, q).wait_send()
+
+    loop(4, s_over.left, 0)
 
     @pl.when(is_root)
     def _():
-        loop(3, lambda k: crx(k, xb_me).wait_send())
+        loop(4, s_out.left, 0)
 
 
 SEMS = 160
@@ -506,7 +553,8 @@
             vmem(4, 128, 256), vmem(4, 16, 128, dtype=F32), vmem(4, 16, 128, dtype=F32), vmem(4, 4, 128, 256),
             vmem(2, 8, 64, 256), vmem(2, 8, 64, 256), vmem(2, 64, 256, dtype=F32),
             vmem(2, 64, 256), vmem(2, 64, 256), vmem(2, 8, 64, 256),
-            vmem(4, 4, 128, 256), vmem(4, 4, 128, 256), vmem(8, 32, 1024), vmem(8, 32, 1024),
+            vmem(4, 4, 128, 256), vmem(4, 2, 128, 256), vmem(4, 2, 128, 256), vmem(4, 2, 128, 256),
+            vmem(8, 32, 1024), vmem(8, 32, 1024),
             vmem(8, 32, 256), vmem(8, 32, 256), vmem(4, 128, 256), vmem(4, 128, 256),
             vmem(2, 512, 256), vmem(2, 512, 256), vmem(4, 2, 128, 256), vmem(4, 2, 128, 256),
             vmem(2, 128, 256), vmem(2, 128, 256),

time: 99.3 us -> 94.7 us (0.954)
  Pallas kernels: 92.6 us -> 88 us
    pallas_call x1, Pallas kernels: 92.6 us -> 88 us  [on_device(): pl.pallas_call(kernel, out_shape=tuple((jax.ShapeDtypeStruct(s, BF) for s...]
where the time goes in v3:
time: 94.7 us; the launch traced here: 94.4 us
  Pallas kernels  88 us (93%)
  local copies, waits for them, and re-layouts  5.71 us (6%)
    pallas_call x1, Pallas kernels, on_device(): pl.pallas_call(kernel, out_shape=tuple((jax.ShapeDtypeStruct(s, BF) for s...  88 us
    unnamed x13, local copies, waits for them, and re-layouts  5.71 us

profile of v3, /device:TPU:6, one launch (start us, length us, event | category | flops | bytes accessed | tf_op | source)
XLA Modules:
  0.0 94.4 jit_solution(8673294910801922228)
XLA Ops:
  0.6 0.0 copy-start.3
  0.6 0.7 copy.11.block_job
  1.4 0.0 copy-done.3
  1.4 0.0 copy-start
  1.4 0.8 copy-done
  2.2 0.0 copy-start.1
  2.2 0.8 copy-done.1
  3.1 0.0 copy-start.2
  3.1 0.7 copy-done.2
  3.8 88.0 %shard_map.102 = (bf16[128,256]{1,0:T(8,128)(2,1)S(1)}, bf16[128,1024]{1,0:T(8,128)(2,1)S(1)}, bf16[32,1024]{1,0:T(8,128)(2,1)S(1)}, bf16[32,256]{1,0:T(8,128)(2,1)S(1)}) custom-call(bf16[128,1024]{1,0:T(8,128)(2,1)} %hid.1, bf16[1024,128]{1,0:T(8,128)(2,1)} %w.1, bf16[32,1024]{1,0:T(8,128)(2,1)S(1)} %copy-done, bf16[32,256]{1,0:T(8,128)(2,1)S(1)} %copy-done.2, ...), custom_call_target="tpu_custom_call" | custom-call | flops 3000000000 | bytes 4000000 | tf_op jit(solution)/shard_map/pallas_call | solution.py:546
  91.8 0.6 copy.16
  92.4 0.7 copy.17
  93.1 0.6 copy.18
  93.8 0.6 copy.19
Async XLA Ops:
  0.6 0.8 copy-start.3
  1.4 0.8 copy-start
  2.2 0.8 copy-start.1
  3.1 0.7 copy-start.2
